TPU v7x, 32 devices: a whole 2x2x4 slice. The times are simulated.
32 devices in a mesh: wide: 8 (over y, x, core), narrow: 4 (over z).
Axes of the slice: x: 2, y: 2, z: 4, core: 2. Of those that a mesh axis runs over, the one named last changes fastest.
Arguments:
- wavefunction: float32 [2, 512, 512, 256], P(None, 'wide', 'narrow'), may hold values from -6 to 6
- previous_slope: float32 [2, 512, 512, 256], P(None, 'wide', 'narrow'), may hold values from -6 to 6
- potential: float32 [512, 512, 256], P('wide', 'narrow'), may hold values from 0.5 to 3
- kinetic_one: float32 [512, 512], replicated, as said below
- coupling_one: float32 [512, 512], replicated, as said below
- kinetic_two: float32 [512, 512], P('narrow'), as said below
- coupling_two: float32 [512, 512], P('narrow'), as said below
- kinetic_three: float32 [256, 256], replicated, as said below
- coupling_three: float32 [256, 256], replicated, as said below
Outputs:
- slope: float32 [2, 512, 512, 256], P(None, 'wide', 'narrow')
- next_input: float32 [2, 512, 512, 256], P(None, 'wide', 'narrow')
Inputs may be any that keep to these rules, and one draw needn't show every extreme that they name: kinetic_one is symmetric. coupling_one is symmetric. kinetic_two is symmetric. coupling_two is symmetric. kinetic_three is symmetric. coupling_three is symmetric.
All inputs are finite; a program needn't handle non-finite values.
Results may differ from a plain program's by a relative error of at most 0.00005.
Values sent between devices are 32-bit elements; how exact they have to be, the bound alone decides.
A program may use at most 384 MiB of HBM per device.

v0:
```python
import jax
import jax.numpy as jnp
from jax import lax
from jax.sharding import PartitionSpec as P

half_step = 0.1


def along_one_flat(matrix, field):
    return jnp.einsum("ij,cjm->cim", matrix, field, precision=lax.Precision.HIGHEST)


def along_two(matrix, field):
    return jnp.einsum("ij,ckjl->ckil", matrix, field, precision=lax.Precision.HIGHEST)


def along_three(matrix, field):
    return jnp.einsum("ij,cklj->ckli", matrix, field, precision=lax.Precision.HIGHEST)


def local(
    wavefunction,
    previous_slope,
    potential,
    kinetic_one,
    coupling_one,
    kinetic_two,
    coupling_two,
    kinetic_three,
    coupling_three,
):
    section_in = wavefunction + half_step * previous_slope
    kinetic_last = along_three(kinetic_three, section_in)
    coupled_last = along_three(coupling_three, section_in)
    parts_count, first_rows, second_rows, third_rows = section_in.shape
    pieces = (
        lax.all_gather(section_in, "narrow", axis=2, tiled=True),
        lax.all_gather(coupled_last, "narrow", axis=2, tiled=True),
    )
    kinetic_middle = along_two(kinetic_two, pieces[0])
    coupled_middle = along_two(coupling_two, pieces[1])
    flat_section = section_in.reshape(parts_count, first_rows, second_rows * third_rows)
    flat_coupled = coupled_middle.reshape(parts_count, first_rows, second_rows * third_rows)
    pieces = (
        lax.all_to_all(flat_section, "wide", split_axis=2, concat_axis=1, tiled=True),
        lax.all_to_all(flat_coupled, "wide", split_axis=2, concat_axis=1, tiled=True),
    )
    summed = along_one_flat(kinetic_one, pieces[0]) + along_one_flat(coupling_one, pieces[1])
    flat_terms = lax.all_to_all(summed, "wide", split_axis=1, concat_axis=2, tiled=True)
    first_terms = flat_terms.reshape(parts_count, first_rows, second_rows, third_rows)
    hamil = first_terms + kinetic_middle + kinetic_last + potential[None] * section_in
    slope = jnp.stack([hamil[1], -hamil[0]])
    next_input = wavefunction + half_step * slope
    return (slope, next_input)


def solution(mesh):
    in_specs = (
        P(None, "wide", "narrow", None),
        P(None, "wide", "narrow", None),
        P("wide", "narrow", None),
        P(),
        P(),
        P("narrow", None),
        P("narrow", None),
        P(),
        P(),
    )
    out_specs = (P(None, "wide", "narrow", None), P(None, "wide", "narrow", None))
    return jax.shard_map(local, mesh=mesh, in_specs=in_specs, out_specs=out_specs, check_vma=False)
```

profile of v0, /device:TPU:0, one launch (start us, length us, event | category | flops | bytes accessed | tf_op | source)
XLA Modules:
  0.0 2545.0 jit_solution(13336320669852960135)
XLA Ops:
  7.2 17.5 copy.37
  24.8 17.4 copy.36
  42.2 17.8 multiply_add_fusion.1
  60.1 33.1 %fusion.9 = f32[2,64,128,256]{3,2,1,0:T(8,128)} fusion(f32[2,64,128,256]{2,3,1,0:T(8,128)} %multiply_add_fusion.1, f32[256,256]{1,0:T(8,128)S(1)} %copy-done.3), kind=kOutput, calls=%fused_computation.16 | convolution fusion | flops 12884901888 | bytes 33816576 | tf_op jit(solution)/shard_map/ij,cklj->ckli/dot_general | solution.py:18
  94.0 32.9 %copy.70 = f32[2,64,128,256]{1,0,3,2:T(2,128)} copy(f32[2,64,128,256]{2,3,1,0:T(8,128)} %multiply_add_fusion.1) | data formatting | bytes 33554432 | tf_op jit(solution)/shard_map/reshape | solution.py:42
  126.9 38.9 %reshape.24 = f32[8,1,524288]{2,1,0:T(1,128)} reshape(f32[32768,2,64]{2,1,0:T(2,128)} %bitcast.66) | data formatting | bytes 33554432
  165.7 5.9 all-to-all-start
  171.6 1035.1 %all-gather.3.cloned.1.call-done = f32[2,64,512,256]{3,2,1,0:T(8,128)} async-done(((f32[2,64,128,256]{3,2,1,0:T(8,128)}), f32[2,64,512,256]{3,2,1,0:T(8,128)}) %all-gather.3.cloned.1.call-update) | async-done | bytes 67108880 | tf_op jit(solution)/shard_map/all_gather | solution.py:38
  1206.7 110.7 %convolution_bitcast_fusion = f32[2,64,128,256]{2,3,1,0:T(8,128)} fusion(f32[2,64,512,256]{3,2,1,0:T(8,128)} %all-gather.3.cloned.1.call-done, f32[128,512]{1,0:T(8,128)S(1)} %copy-done.4), kind=kOutput, calls=%fused_computation.8 | convolution fusion | flops 25769803776 | bytes 84148224 | tf_op jit(solution)/shard_map/ij,ckjl->ckil/dot_general | solution.py:14
  1317.4 31.2 %copy.73 = f32[2,64,128,256]{1,0,3,2:T(2,128)} copy(f32[2,64,128,256]{2,3,1,0:T(8,128)} %convolution_bitcast_fusion) | data formatting | bytes 33554432 | tf_op jit(solution)/shard_map/reshape | solution.py:43
  1348.6 38.4 %reshape.26 = f32[8,1,524288]{2,1,0:T(1,128)} reshape(f32[32768,2,64]{2,1,0:T(2,128)} %bitcast.63) | data formatting | bytes 33554432
  1393.4 50.2 %reduce = f32[8,524288]{1,0:T(8,128)} reduce(f32[8,1,524288]{2,1,0:T(1,128)} %all-to-all-done, f32[]{:T(128)} %broadcast.7), dimensions={1}, to_apply=%all_to_all.37.reduce_sub_computation | reduce | bytes 33554436 | tf_op jit(solution)/shard_map/all_to_all | solution.py:45
  1443.6 69.6 %reshape.25 = f32[32768,2,64]{2,1,0:T(2,128)} reshape(f32[8,524288]{1,0:T(8,128)} %reduce) | data formatting | bytes 33554432
  1513.2 42.0 %copy.72 = f32[2,64,8,4096]{3,1,2,0:T(8,128)} copy(f32[2,64,8,4096]{1,0,3,2:T(2,128)} %bitcast.64) | data formatting | bytes 33554432 | tf_op jit(solution)/shard_map/all_to_all | solution.py:45
  1555.2 57.5 %fusion.3 = f32[2,4096,512]{2,1,0:T(8,128)} fusion(f32[2,512,4096]{2,1,0:T(8,128)} %bitcast.68, f32[512,512]{1,0:T(8,128)S(1)} %copy-done), kind=kOutput, calls=%fused_computation.10 | convolution fusion | flops 25769803776 | bytes 34603008 | tf_op jit(solution)/shard_map/ij,cjm->cim/dot_general | solution.py:10
  1612.7 50.1 %reduce.1 = f32[8,524288]{1,0:T(8,128)} reduce(f32[8,1,524288]{2,1,0:T(1,128)} %all-to-all-done.1, f32[]{:T(128)} %broadcast.7), dimensions={1}, to_apply=%all_to_all.41.reduce_sub_computation | reduce | bytes 33554436 | tf_op jit(solution)/shard_map/all_to_all | solution.py:46
  1662.8 68.9 %reshape.27 = f32[32768,2,64]{2,1,0:T(2,128)} reshape(f32[8,524288]{1,0:T(8,128)} %reduce.1) | data formatting | bytes 33554432
  1731.7 42.1 %copy.75 = f32[2,64,8,4096]{3,1,2,0:T(8,128)} copy(f32[2,64,8,4096]{1,0,3,2:T(2,128)} %bitcast.65) | data formatting | bytes 33554432 | tf_op jit(solution)/shard_map/all_to_all | solution.py:46
  1773.8 58.8 %add_bitcast_fusion = f32[2,512,4096]{1,2,0:T(8,128)} fusion(f32[2,4096,512]{2,1,0:T(8,128)} %fusion.3, f32[2,512,4096]{2,1,0:T(8,128)} %bitcast.67, f32[512,512]{1,0:T(8,128)S(1)} %copy-done.2), kind=kOutput, calls=%fused_computation.5 | convolution fusion | flops 25773998080 | bytes 51380224 | tf_op jit(solution)/shard_map/ij,cjm->cim/dot_general | solution.py:10
  1832.6 25.5 %copy.50 = f32[2,512,4096]{2,0,1:T(2,128)} copy(f32[2,512,4096]{1,2,0:T(8,128)} %add_bitcast_fusion) | data formatting | bytes 33554432 | tf_op jit(solution)/shard_map/add | solution.py:48
  1863.9 9.1 copy.56
  1873.0 444.2 %all-gather.5.cloned.1.call-done = f32[2,64,512,256]{2,3,1,0:T(8,128)} async-done(((f32[2,64,128,256]{2,3,1,0:T(8,128)}), f32[2,64,512,256]{2,3,1,0:T(8,128)}) %all-gather.5.cloned.1.call-update) | async-done | bytes 67108880 | tf_op jit(solution)/shard_map/all_gather | solution.py:37
  2317.2 59.5 %fusion.6 = f32[2,64,256,128]{3,2,1,0:T(8,128)} fusion(f32[2,64,512,256]{2,3,1,0:T(8,128)} %all-gather.5.cloned.1.call-done, f32[128,512]{1,0:T(8,128)S(1)} %copy-done.5), kind=kOutput, calls=%fused_computation.13 | convolution fusion | flops 25769803776 | bytes 84148224 | tf_op jit(solution)/shard_map/ij,ckjl->ckil/dot_general | solution.py:14
  2376.7 15.2 copy.51
  2391.9 19.5 copy.52
  2411.4 18.0 reshape.17
  2429.4 17.5 copy.53
  2446.9 33.1 %fusion.1 = f32[2,64,128,256]{2,3,1,0:T(8,128)} fusion(f32[2,64,128,256]{2,3,1,0:T(8,128)} %copy.53, f32[2,64,256,128]{3,2,1,0:T(8,128)} %fusion.6, f32[2,64,128,256]{2,3,1,0:T(8,128)} %multiply_add_fusion.1, f32[64,128,256]{1,2,0:T(8,128)} %copy.56, f32[256,256]{1,0:T(8,128)S(1)} %copy-done.6), kind=kOutput, calls=%fused_computation.3 | convolution fusion | flops 12901679104 | bytes 75759616 | tf_op jit(solution)/shard_map/ij,cklj->ckli/dot_general | solution.py:18
  2480.0 6.5 fusion.11
  2486.5 16.4 multiply_add_fusion
  2502.9 17.5 copy.58
  2520.4 17.6 copy.59
  (24 shorter events, 12.9 us)
Async XLA Ops:
  7.2 1548.0 %copy-start = (f32[512,512]{1,0:T(8,128)S(1)}, f32[512,512]{1,0:T(8,128)}, u32[]{:S(2)}) copy-start(f32[512,512]{1,0:T(8,128)} %param.12) | copy-start | bytes 3145732
  7.2 1199.5 %all-gather.3.cloned.1.call-start = ((), (), s32[]{:S(2)}) async-start(), calls=%async_computation.3 | async-start | bytes 83886080 | tf_op jit(solution)/shard_map/all_gather | solution.py:38
  42.2 17.8 copy-start.3
  93.2 2224.0 %all-gather.5.cloned.1.call-start = ((), (), s32[]{:S(2)}) async-start(), calls=%async_computation.4 | async-start | bytes 83886080 | tf_op jit(solution)/shard_map/all_gather | solution.py:37
  165.7 1041.0 %copy-start.4 = (f32[128,512]{1,0:T(8,128)S(1)}, f32[128,512]{1,0:T(8,128)}, u32[]{:S(2)}) copy-start(f32[128,512]{1,0:T(8,128)} %param.15) | copy-start | bytes 786436
  165.7 1221.3 %all-to-all-start = ((f32[8,1,524288]{2,1,0:T(1,128)}), f32[8,1,524288]{2,1,0:T(1,128)}, u32[]{:S(2)}, u32[]{:S(2)}) async-start(f32[8,1,524288]{2,1,0:T(1,128)} %reshape.24), calls=%async_computation | async-start | bytes 33554432 | tf_op jit(solution)/shard_map/all_to_all | solution.py:45
  1387.1 225.7 %all-to-all-start.1 = ((f32[8,1,524288]{2,1,0:T(1,128)}), f32[8,1,524288]{2,1,0:T(1,128)}, u32[]{:S(2)}, u32[]{:S(2)}) async-start(f32[8,1,524288]{2,1,0:T(1,128)} %reshape.26), calls=%async_computation.1 | async-start | bytes 33554432 | tf_op jit(solution)/shard_map/all_to_all | solution.py:46
  1731.7 42.1 %copy-start.2 = (f32[512,512]{1,0:T(8,128)S(1)}, f32[512,512]{1,0:T(8,128)}, u32[]{:S(2)}) copy-start(f32[512,512]{1,0:T(8,128)} %param.13) | copy-start | bytes 3145732
  1858.2 518.5 %all-to-all-start.2 = ((f32[2,512,4096]{2,0,1:T(2,128)}), f32[2,512,4096]{2,0,1:T(2,128)}, u32[]{:S(2)}, u32[]{:S(2)}) async-start(f32[2,512,4096]{2,0,1:T(2,128)} %copy.50), calls=%async_computation.2 | async-start | bytes 33554432 | tf_op jit(solution)/shard_map/all_to_all | solution.py:49
  1863.9 453.3 %copy-start.5 = (f32[128,512]{1,0:T(8,128)S(1)}, f32[128,512]{1,0:T(8,128)}, u32[]{:S(2)}) copy-start(f32[128,512]{1,0:T(8,128)} %param.14) | copy-start | bytes 786436
  2429.4 17.5 copy-start.6
  2520.4 17.6 copy-start.1
Sparse Core Ops, SparseCore 0:
  93.3 1113.3 all-gather.2
  1208.9 1108.3 all-gather.4
where the time goes:
time: 2560 us; the launch traced here: 2550 us
  waiting for transfers between devices  1480 us (58%)
  local copies, waits for them, and re-layouts  539 us (21%)
  matrix products  353 us (14%)
  other arithmetic  141 us (6%)
    all_gather x1, waiting for transfers between devices, local(): lax.all_gather(coupled_last, 'narrow', axis=2, tiled=True)  1040 us
    all_gather x1, waiting for transfers between devices, local(): lax.all_gather(section_in, 'narrow', axis=2, tiled=True)  444 us
    unnamed x23, local copies, waits for them, and re-layouts  295 us
    dot_general x2, matrix products, along_two(): jnp.einsum('ij,ckjl->ckil', matrix, field, precision=lax.Precision.HIGHEST)  170 us
    dot_general x2, matrix products, along_one_flat(): jnp.einsum('ij,cjm->cim', matrix, field, precision=lax.Precision.HIGHEST)  116 us
    dot_general x2, matrix products, along_three(): jnp.einsum('ij,cklj->ckli', matrix, field, precision=lax.Precision.HIGHEST)  66.2 us
  transfers between devices with their start and end apart: 5, of which 2 were waited for; matrix products, arithmetic and copies ran while one was open for 31% of the time, Pallas kernels for 0%

commit v1 on v0

v1 whole, which is shorter than its diff:
```python
import jax
import jax.numpy as jnp
from jax import lax
from jax.sharding import PartitionSpec as P

half_step = 0.1
HIGH = lax.Precision.HIGH


def along_one(matrix, field):
    return jnp.einsum("ij,jkl->ikl", matrix, field, precision=HIGH)


def along_two(matrix, field):
    return jnp.einsum("ij,kjl->kil", matrix, field, precision=HIGH)


def along_three(matrix, field):
    return jnp.einsum("ij,klj->kli", matrix, field, precision=HIGH)


def to_whole_one(field, wide):
    rows, second, third = field.shape
    blocks = field.reshape(rows, wide, second // wide, third).transpose(1, 0, 2, 3)
    moved = lax.all_to_all(blocks, "wide", split_axis=0, concat_axis=0, tiled=True)
    return moved.reshape(wide * rows, second // wide, third)


def from_whole_one(field, wide):
    rows, second, third = field.shape
    blocks = field.reshape(wide, rows // wide, second, third)
    moved = lax.all_to_all(blocks, "wide", split_axis=0, concat_axis=0, tiled=True)
    return moved.transpose(1, 0, 2, 3).reshape(rows // wide, wide * second, third)


def local(
    wide,
    wavefunction,
    previous_slope,
    potential,
    kinetic_one,
    coupling_one,
    kinetic_two,
    coupling_two,
    kinetic_three,
    coupling_three,
):
    sections = [wavefunction[c] + half_step * previous_slope[c] for c in range(2)]
    gathered = [lax.all_gather(s, "narrow", axis=1, tiled=True) for s in sections]
    whole = [to_whole_one(s, wide) for s in sections]
    base = [along_three(kinetic_three, s) + potential * s for s in sections]
    kinetic = [along_one(kinetic_one, s) for s in whole]
    hamil = []
    for c in range(2):
        coupled = along_three(coupling_three, along_two(coupling_two, gathered[c]))
        summed = kinetic[c] + along_one(coupling_one, to_whole_one(coupled, wide))
        hamil.append(from_whole_one(summed, wide) + along_two(kinetic_two, gathered[c]) + base[c])
    slope = jnp.stack([hamil[1], -hamil[0]])
    next_input = wavefunction + half_step * slope
    return (slope, next_input)


def solution(mesh):
    wide = mesh.shape["wide"]
    in_specs = (
        P(None, "wide", "narrow", None),
        P(None, "wide", "narrow", None),
        P("wide", "narrow", None),
        P(),
        P(),
        P("narrow", None),
        P("narrow", None),
        P(),
        P(),
    )
    out_specs = (P(None, "wide", "narrow", None), P(None, "wide", "narrow", None))

    def body(*arrays):
        return local(wide, *arrays)

    return jax.shard_map(body, mesh=mesh, in_specs=in_specs, out_specs=out_specs, check_vma=False)
```

time: 2560 us -> 1660 us (0.65)
  local copies, waits for them, and re-layouts: 539 us -> 192 us
  waiting for transfers between devices: 1480 us -> 1150 us
  matrix products: 353 us -> 222 us
  other arithmetic: 141 us -> 40.3 us
    all_gather x2, waiting for transfers between devices: 1480 us -> 955 us  [local(): lax.all_gather(s, 'narrow', axis=1, tiled=True)]
    unnamed x23 -> x20, local copies, waits for them, and re-layouts: 295 us -> 79.6 us
    all_to_all x3 -> x6, waiting for transfers between devices: 0.01 us -> 194 us  [the longest x4 123 us: to_whole_one(): lax.all_to_all(blocks, 'wide', split_axis=0, concat_axis=0, tiled=True)]
    dot_general x6 -> x12, matrix products: 353 us -> 222 us  [the longest x4 88.3 us: along_two(): return jnp.einsum('ij,kjl->kil', matrix, field, precision=HIGH)]
    all_to_all x5 -> x0, local copies, waits for them, and re-layouts: 119 us -> none  [the longest x2 42.6 us: local(): lax.all_to_all(flat_section, 'wide', split_axis=2, concat_axis=1, tiled=T...]
    all_to_all x2 -> x0, other arithmetic: 100 us -> none  [the longest x1 50.2 us: local(): lax.all_to_all(flat_section, 'wide', split_axis=2, concat_axis=1, tiled=T...]
    reshape x4, local copies, waits for them, and re-layouts: 99.6 us -> 26.7 us  [the longest x2 18 us: from_whole_one(): moved.transpose(1, 0, 2, 3).reshape(rows // wide, wide * second, third)]
    transpose x0 -> x4, local copies, waits for them, and re-layouts: none -> 35.8 us  [the longest x2 19.6 us: to_whole_one(): field.reshape(rows, wide, second // wide, third).transpose(1, 0, 2, 3)]
  transfers between devices with their start and end apart: 5 -> 8, of which waited for: 2 -> 6; matrix products, arithmetic and copies ran while one was open for 31% -> 17% of each run, Pallas kernels for 0% -> 0%
where the time goes in v1:
time: 1660 us; the launch traced here: 1650 us
  waiting for transfers between devices  1150 us (69%)
  matrix products  222 us (13%)
  local copies, waits for them, and re-layouts  192 us (12%)
  other arithmetic  40.3 us (2%)
  starting transfers between devices  31.5 us (2%)
    all_gather x2, waiting for transfers between devices, local(): lax.all_gather(s, 'narrow', axis=1, tiled=True)  955 us
    all_to_all x4, waiting for transfers between devices, to_whole_one(): lax.all_to_all(blocks, 'wide', split_axis=0, concat_axis=0, tiled=True)  123 us
    dot_general x4, matrix products, along_two(): return jnp.einsum('ij,kjl->kil', matrix, field, precision=HIGH)  88.3 us
    unnamed x20, local copies, waits for them, and re-layouts  79.6 us
    dot_general x4, matrix products, along_one(): return jnp.einsum('ij,jkl->ikl', matrix, field, precision=HIGH)  75.7 us
    all_to_all x2, waiting for transfers between devices, from_whole_one(): lax.all_to_all(blocks, 'wide', split_axis=0, concat_axis=0, tiled=True)  71.4 us
    dot_general x4, matrix products, along_three(): return jnp.einsum('ij,klj->kli', matrix, field, precision=HIGH)  57.8 us
  transfers between devices with their start and end apart: 8, of which 6 were waited for; matrix products, arithmetic and copies ran while one was open for 17% of the time, Pallas kernels for 0%

profile of v1, /device:TPU:0, one launch (start us, length us, event | category | flops | bytes accessed | tf_op | source)
XLA Modules:
  0.0 1650.0 jit_solution(9052472090214704067)
XLA Ops:
  7.2 11.1 fusion.51
  18.4 9.0 copy.96
  36.4 17.4 %copy.59 = f32[2,64,128,256]{2,3,1,0:T(8,128)} copy(f32[2,64,128,256]{3,2,1,0:T(8,128)} %param.9) | data formatting | bytes 33554432 | tf_op args[0]
  53.8 19.2 %slice_add_fusion.1 = (f32[1,64,128,256]{2,3,1,0:T(8,128)}, f32[1,64,128,256]{2,3,1,0:T(8,128)}) fusion(f32[2,64,128,256]{2,3,1,0:T(8,128)} %copy.59, f32[1,64,128,256]{2,3,1,0:T(8,128)} %copy.96, f32[1,64,128,256]{2,3,1,0:T(8,128)} %copy.97), kind=kLoop, calls=%fused_computation.11 | loop fusion | flops 8388608 | bytes 50331648 | tf_op jit(solution)/shard_map/add | solution.py:48
  73.8 9.1 copy.61
  82.9 11.4 copy.62
  99.3 9.1 copy.75
  116.6 77.2 %all-to-all-done = f32[8,64,16,256]{3,2,1,0:T(8,128)} async-done(((f32[8,64,16,256]{3,2,1,0:T(8,128)}), f32[8,64,16,256]{3,2,1,0:T(8,128)}, u32[]{:S(2)}, u32[]{:S(2)}) %all-to-all-start) | async-done | bytes 8388640 | tf_op jit(solution)/shard_map/all_to_all | solution.py:25
  199.0 437.8 %all-gather.5.cloned.1.call-done = f32[1,64,512,256]{2,3,1,0:T(8,128)} async-done(((f32[1,64,128,256]{2,3,1,0:T(8,128)}), f32[1,64,512,256]{2,3,1,0:T(8,128)}) %all-gather.5.cloned.1.call-update) | async-done | bytes 33554448 | tf_op jit(solution)/shard_map/all_gather | solution.py:49
  636.8 24.7 %fusion.6 = f32[64,256,128]{2,1,0:T(8,128)} fusion(f32[1,64,512,256]{2,3,1,0:T(8,128)} %all-gather.5.cloned.1.call-done, f32[128,512]{1,0:T(8,128)S(1)} %copy-done.3), kind=kOutput, calls=%fused_computation.6 | convolution fusion | flops 6442450944 | bytes 42205184 | tf_op jit(solution)/shard_map/ij,kjl->kil/dot_general | solution.py:15
  661.5 9.5 fusion.21
  680.6 516.9 %all-gather.7.cloned.1.call-done = f32[1,64,512,256]{2,3,1,0:T(8,128)} async-done(((f32[1,64,128,256]{2,3,1,0:T(8,128)}), f32[1,64,512,256]{2,3,1,0:T(8,128)}) %all-gather.7.cloned.1.call-update) | async-done | bytes 33554448 | tf_op jit(solution)/shard_map/all_gather | solution.py:49
  1197.5 21.2 %fusion.2 = f32[64,256,128]{2,1,0:T(8,128)} fusion(f32[1,64,512,256]{2,3,1,0:T(8,128)} %all-gather.7.cloned.1.call-done, f32[128,512]{1,0:T(8,128)S(1)} %copy-done.3), kind=kOutput, calls=%fused_computation.2 | convolution fusion | flops 6442450944 | bytes 42205184 | tf_op jit(solution)/shard_map/ij,kjl->kil/dot_general | solution.py:15
  1218.7 9.4 fusion.14
  1237.9 17.9 %fusion.27 = f32[16,256,512]{2,1,0:T(8,128)S(1)} fusion(f32[512,16,256]{2,1,0:T(8,128)} %bitcast.10, f32[512,512]{1,0:T(8,128)S(1)} %copy-done), kind=kOutput, calls=%fused_computation.36 | convolution fusion | flops 6442450944 | bytes 17825792 | tf_op jit(solution)/shard_map/ij,jkl->ikl/dot_general | solution.py:11
  1255.8 19.9 %add_bitcast_fusion.1 = f32[512,16,256]{0,2,1:T(8,128)} fusion(f32[16,256,512]{2,1,0:T(8,128)S(1)} %fusion.27, f32[512,16,256]{2,1,0:T(8,128)} %bitcast.2, f32[512,512]{1,0:T(8,128)S(1)} %copy-done.2), kind=kOutput, calls=%fused_computation.42 | convolution fusion | flops 6444548096 | bytes 26214400 | tf_op jit(solution)/shard_map/ij,jkl->ikl/dot_general | solution.py:11
  1275.7 10.4 copy.67
  1286.1 45.8 %all-to-all-done.4 = f32[8,64,16,256]{3,2,1,0:T(8,128)} async-done(((f32[8,64,16,256]{3,2,1,0:T(8,128)}), f32[8,64,16,256]{3,2,1,0:T(8,128)}, u32[]{:S(2)}, u32[]{:S(2)}) %all-to-all-start.4) | async-done | bytes 8388640 | tf_op jit(solution)/shard_map/all_to_all | solution.py:25
  1337.1 17.8 %fusion.23 = f32[16,256,512]{2,1,0:T(8,128)S(1)} fusion(f32[512,16,256]{2,1,0:T(8,128)} %bitcast.28, f32[512,512]{1,0:T(8,128)S(1)} %copy-done), kind=kOutput, calls=%fused_computation.31 | convolution fusion | flops 6442450944 | bytes 17825792 | tf_op jit(solution)/shard_map/ij,jkl->ikl/dot_general | solution.py:11
  1355.0 20.1 %add_bitcast_fusion = f32[512,16,256]{0,2,1:T(8,128)} fusion(f32[16,256,512]{2,1,0:T(8,128)S(1)} %fusion.23, f32[512,16,256]{2,1,0:T(8,128)} %bitcast.23, f32[512,512]{1,0:T(8,128)S(1)} %copy-done.2), kind=kOutput, calls=%fused_computation.41 | convolution fusion | flops 6444548096 | bytes 26214400 | tf_op jit(solution)/shard_map/ij,jkl->ikl/dot_general | solution.py:11
  1375.0 10.3 copy.81
  1385.3 45.9 %all-to-all-done.2 = f32[8,64,16,256]{3,2,1,0:T(8,128)} async-done(((f32[8,64,16,256]{3,2,1,0:T(8,128)}), f32[8,64,16,256]{3,2,1,0:T(8,128)}, u32[]{:S(2)}, u32[]{:S(2)}) %all-to-all-start.2) | async-done | bytes 8388640 | tf_op jit(solution)/shard_map/all_to_all | solution.py:32
  1436.7 9.0 copy.71
  1445.7 21.2 %fusion.4 = f32[64,256,128]{2,1,0:T(8,128)} fusion(f32[1,64,512,256]{2,3,1,0:T(8,128)} %all-gather.5.cloned.1.call-done, f32[128,512]{1,0:T(8,128)S(1)} %copy-done.5), kind=kOutput, calls=%fused_computation.4 | convolution fusion | flops 6442450944 | bytes 42205184 | tf_op jit(solution)/shard_map/ij,kjl->kil/dot_general | solution.py:15
  1466.9 21.3 %fusion = f32[64,256,128]{2,1,0:T(8,128)} fusion(f32[1,64,512,256]{2,3,1,0:T(8,128)} %all-gather.7.cloned.1.call-done, f32[128,512]{1,0:T(8,128)S(1)} %copy-done.5), kind=kOutput, calls=%fused_computation | convolution fusion | flops 6442450944 | bytes 42205184 | tf_op jit(solution)/shard_map/ij,kjl->kil/dot_general | solution.py:15
  1505.2 25.5 %all-to-all-done.5 = f32[8,64,16,256]{3,2,1,0:T(8,128)} async-done(((f32[8,64,16,256]{3,2,1,0:T(8,128)}), f32[8,64,16,256]{3,2,1,0:T(8,128)}, u32[]{:S(2)}, u32[]{:S(2)}) %all-to-all-start.5) | async-done | bytes 8388640 | tf_op jit(solution)/shard_map/all_to_all | solution.py:32
  1538.8 9.0 copy.83
  1547.8 19.7 %fusion.20 = f32[1,64,128,256]{2,3,1,0:T(8,128)} fusion(f32[64,128,256]{1,2,0:T(8,128)} %copy.71, f32[1,64,128,256]{2,3,1,0:T(8,128)} %get-tuple-element.10, f32[64,128,256]{1,2,0:T(8,128)} %copy.69, f32[64,256,128]{2,1,0:T(8,128)} %fusion.4, f32[256,256]{1,0:T(8,128)S(1)} %copy-done.6), kind=kOutput, calls=%fused_computation.27 | convolution fusion | flops 3229614080 | bytes 42205184 | tf_op jit(solution)/shard_map/ij,klj->kli/dot_general | solution.py:19
  1567.5 19.3 %fusion.13 = f32[1,64,128,256]{2,3,1,0:T(8,128)} fusion(f32[64,128,256]{1,2,0:T(8,128)} %copy.71, f32[1,64,128,256]{2,3,1,0:T(8,128)} %get-tuple-element.11, f32[64,128,256]{1,2,0:T(8,128)} %copy.83, f32[64,256,128]{2,1,0:T(8,128)} %fusion, f32[256,256]{1,0:T(8,128)S(1)} %copy-done.6), kind=kOutput, calls=%fused_computation.18 | convolution fusion | flops 3231711232 | bytes 42205184 | tf_op jit(solution)/shard_map/ij,klj->kli/dot_general | solution.py:19
  1586.8 21.1 %multiply_add_fusion = (f32[2,64,128,256]{2,3,1,0:T(8,128)}, f32[2,64,128,256]{2,3,1,0:T(8,128)}) fusion(f32[2,64,128,256]{2,3,1,0:T(8,128)} %copy.59, f32[1,64,128,256]{2,3,1,0:T(8,128)} %fusion.13, f32[1,64,128,256]{2,3,1,0:T(8,128)} %fusion.20), kind=kLoop, calls=%fused_computation.9 | loop fusion | flops 12582912 | bytes 67108864 | tf_op jit(solution)/shard_map/add | solution.py:59
  1607.9 17.5 %copy.88 = f32[2,64,128,256]{3,2,1,0:T(8,128)} copy(f32[2,64,128,256]{2,3,1,0:T(8,128)} %get-tuple-element.9) | data formatting | bytes 33554432
  1625.3 17.6 %copy.89 = f32[2,64,128,256]{3,2,1,0:T(8,128)} copy(f32[2,64,128,256]{2,3,1,0:T(8,128)} %get-tuple-element.8) | data formatting | bytes 33554432
  (33 shorter events, 83.3 us)
Async XLA Ops:
  7.2 1230.7 %copy-start = (f32[512,512]{1,0:T(8,128)S(1)}, f32[512,512]{1,0:T(8,128)}, u32[]{:S(2)}) copy-start(f32[512,512]{1,0:T(8,128)} %param.13) | copy-start | bytes 3145732
  7.2 629.6 %all-gather.5.cloned.1.call-start = ((), (), s32[]{:S(2)}) async-start(), calls=%async_computation.6 | async-start | bytes 41943040 | tf_op jit(solution)/shard_map/all_gather | solution.py:49
  73.1 1124.4 %all-gather.7.cloned.1.call-start = ((), (), s32[]{:S(2)}) async-start(), calls=%async_computation.7 | async-start | bytes 41943040 | tf_op jit(solution)/shard_map/all_gather | solution.py:49
  94.3 99.5 %all-to-all-start = ((f32[8,64,16,256]{3,2,1,0:T(8,128)}), f32[8,64,16,256]{3,2,1,0:T(8,128)}, u32[]{:S(2)}, u32[]{:S(2)}) async-start(f32[8,64,16,256]{3,2,1,0:T(8,128)} %copy.62), calls=%async_computation | async-start | bytes 16777216 | tf_op jit(solution)/shard_map/all_to_all | solution.py:25
  116.6 520.2 %copy-start.3 = (f32[128,512]{1,0:T(8,128)S(1)}, f32[128,512]{1,0:T(8,128)}, u32[]{:S(2)}) copy-start(f32[128,512]{1,0:T(8,128)} %param.15) | copy-start | bytes 786436
  193.8 481.5 %all-to-all-start.3 = ((f32[8,64,16,256]{3,2,1,0:T(8,128)}), f32[8,64,16,256]{3,2,1,0:T(8,128)}, u32[]{:S(2)}, u32[]{:S(2)}) async-start(f32[8,64,16,256]{3,2,1,0:T(8,128)} %copy.76), calls=%async_computation.3 | async-start | bytes 16777216 | tf_op jit(solution)/shard_map/all_to_all | solution.py:25
  199.0 462.5 %copy-start.4 = (f32[256,256]{1,0:T(8,128)S(1)}, f32[256,256]{1,0:T(8,128)}, u32[]{:S(2)}) copy-start(f32[256,256]{1,0:T(8,128)} %param.17) | copy-start | bytes 786436
  675.3 557.1 %all-to-all-start.1 = ((f32[8,64,16,256]{3,2,1,0:T(8,128)}), f32[8,64,16,256]{3,2,1,0:T(8,128)}, u32[]{:S(2)}, u32[]{:S(2)}) async-start(f32[8,64,16,256]{3,2,1,0:T(8,128)} %bitcast.113), calls=%async_computation.1 | async-start | bytes 16777216 | tf_op jit(solution)/shard_map/all_to_all | solution.py:25
  1232.5 99.5 %all-to-all-start.4 = ((f32[8,64,16,256]{3,2,1,0:T(8,128)}), f32[8,64,16,256]{3,2,1,0:T(8,128)}, u32[]{:S(2)}, u32[]{:S(2)}) async-start(f32[8,64,16,256]{3,2,1,0:T(8,128)} %bitcast.114), calls=%async_computation.4 | async-start | bytes 16777216 | tf_op jit(solution)/shard_map/all_to_all | solution.py:25
  1237.9 17.9 %copy-start.2 = (f32[512,512]{1,0:T(8,128)S(1)}, f32[512,512]{1,0:T(8,128)}, u32[]{:S(2)}) copy-start(f32[512,512]{1,0:T(8,128)} %param.12) | copy-start | bytes 3145732
  1331.9 99.3 %all-to-all-start.2 = ((f32[8,64,16,256]{3,2,1,0:T(8,128)}), f32[8,64,16,256]{3,2,1,0:T(8,128)}, u32[]{:S(2)}, u32[]{:S(2)}) async-start(f32[8,64,16,256]{3,2,1,0:T(8,128)} %bitcast.115), calls=%async_computation.2 | async-start | bytes 16777216 | tf_op jit(solution)/shard_map/all_to_all | solution.py:32
  1431.2 99.5 %all-to-all-start.5 = ((f32[8,64,16,256]{3,2,1,0:T(8,128)}), f32[8,64,16,256]{3,2,1,0:T(8,128)}, u32[]{:S(2)}, u32[]{:S(2)}) async-start(f32[8,64,16,256]{3,2,1,0:T(8,128)} %bitcast.112), calls=%async_computation.5 | async-start | bytes 16777216 | tf_op jit(solution)/shard_map/all_to_all | solution.py:32
  1436.7 9.0 copy-start.5
  1538.8 9.0 copy-start.6
  1625.3 17.6 %copy-start.1 = (f32[512,512]{1,0:T(8,128)S(1)}, f32[512,512]{1,0:T(8,128)}, u32[]{:S(2)}) copy-start(f32[512,512]{1,0:T(8,128)} %param.13) | copy-start | bytes 3145732
Sparse Core Ops, SparseCore 0:
  73.2 563.5 all-gather.4
  638.4 559.0 all-gather.6

commit v2 on v1

--- a/solution.py
+++ b/solution.py
@@ -4,6 +4,7 @@
 from jax.sharding import PartitionSpec as P
 
 half_step = 0.1
+pieces = 2
 HIGH = lax.Precision.HIGH
 
 
@@ -33,6 +34,33 @@
     return moved.transpose(1, 0, 2, 3).reshape(rows // wide, wide * second, third)
 
 
+def two_weights(kinetic_two, coupling_two):
+    me = lax.axis_index("narrow")
+    size = kinetic_two.shape[0]
+    hub = jnp.where((me == 1) | (me == 2), 1.0, 0.0)
+    slots = (me, jnp.maximum(me - 1, 0), jnp.minimum(me + 1, 3), jnp.where(me == 1, 3, 0))
+    result = []
+    for matrix in (coupling_two, kinetic_two):
+        ends = lax.ppermute(matrix, "narrow", [(0, 1), (3, 2)])
+        for rows in (ends, matrix * hub):
+            result.append(jnp.concatenate([lax.dynamic_slice_in_dim(rows, slot * size, size, 1) for slot in slots], axis=1))
+    return result
+
+
+def middle_terms(weights, section):
+    me = lax.axis_index("narrow")
+    lower = lax.ppermute(section, "narrow", [(0, 1), (1, 2)])
+    upper = lax.ppermute(section, "narrow", [(3, 2), (2, 1)])
+    far = lax.ppermute(jnp.where(me == 1, lower, upper), "narrow", [(1, 2), (2, 1)])
+    field = jnp.concatenate([section, lower, upper, far], axis=1)
+    coupling_ends, coupling_own, kinetic_ends, kinetic_own = weights
+    result = []
+    for ends, own in ((coupling_ends, coupling_own), (kinetic_ends, kinetic_own)):
+        received = lax.ppermute(along_two(ends, field), "narrow", [(1, 0), (2, 3)])
+        result.append(along_two(own, field) + received)
+    return result
+
+
 def local(
     wide,
     wavefunction,
@@ -45,16 +73,20 @@
     kinetic_three,
     coupling_three,
 ):
+    rows = wavefunction.shape[1]
+    half = rows // pieces
     sections = [wavefunction[c] + half_step * previous_slope[c] for c in range(2)]
-    gathered = [lax.all_gather(s, "narrow", axis=1, tiled=True) for s in sections]
+    weights = two_weights(kinetic_two, coupling_two)
+    second = [[middle_terms(weights, s[p * half:(p + 1) * half]) for p in range(pieces)] for s in sections]
     whole = [to_whole_one(s, wide) for s in sections]
+    kinetic = [along_one(kinetic_one, s) for s in whole]
     base = [along_three(kinetic_three, s) + potential * s for s in sections]
-    kinetic = [along_one(kinetic_one, s) for s in whole]
     hamil = []
     for c in range(2):
-        coupled = along_three(coupling_three, along_two(coupling_two, gathered[c]))
+        coupled = jnp.concatenate([along_three(coupling_three, terms[0]) for terms in second[c]])
         summed = kinetic[c] + along_one(coupling_one, to_whole_one(coupled, wide))
-        hamil.append(from_whole_one(summed, wide) + along_two(kinetic_two, gathered[c]) + base[c])
+        middle = jnp.concatenate([terms[1] for terms in second[c]])
+        hamil.append(from_whole_one(summed, wide) + middle + base[c])
     slope = jnp.stack([hamil[1], -hamil[0]])
     next_input = wavefunction + half_step * slope
     return (slope, next_input)

time: 1660 us -> 1560 us (0.940)
  waiting for transfers between devices: 1150 us -> 853 us
  matrix products: 222 us -> 315 us
  starting transfers between devices: 31.5 us -> 94.2 us
  other arithmetic: 40.3 us -> 77.8 us
    all_gather x2 -> x0, waiting for transfers between devices: 955 us -> none  [local(): lax.all_gather(s, 'narrow', axis=1, tiled=True)]
    ppermute x0 -> x22, waiting for transfers between devices: none -> 784 us  [the longest x8 525 us: middle_terms(): received = lax.ppermute(along_two(ends, field), 'narrow', [(1, 0), (2, 3)])]
    dot_general x4 -> x16, matrix products: 88.3 us -> 176 us  [along_two(): return jnp.einsum('ij,kjl->kil', matrix, field, precision=HIGH)]
    all_to_all x4, waiting for transfers between devices: 123 us -> 45.7 us  [to_whole_one(): lax.all_to_all(blocks, 'wide', split_axis=0, concat_axis=0, tiled=True)]
    ppermute x0 -> x22, starting transfers between devices: none -> 63.5 us  [the longest x4 27.1 us: middle_terms(): lower = lax.ppermute(section, 'narrow', [(0, 1), (1, 2)])]
    all_to_all x2, waiting for transfers between devices: 71.4 us -> 23.8 us  [from_whole_one(): lax.all_to_all(blocks, 'wide', split_axis=0, concat_axis=0, tiled=True)]
    select_n x0 -> x4, other arithmetic: none -> 17.5 us  [middle_terms(): jnp.where(me == 1, lower, upper)]
    dot_general x4 -> x6, matrix products: 57.8 us -> 62.9 us  [along_three(): return jnp.einsum('ij,klj->kli', matrix, field, precision=HIGH)]
  transfers between devices with their start and end apart: 8 -> 28, of which waited for: 6 -> 14; matrix products, arithmetic and copies ran while one was open for 17% -> 26% of each run, Pallas kernels for 0% -> 0%
where the time goes in v2:
time: 1560 us; the launch traced here: 1540 us
  waiting for transfers between devices  853 us (55%)
  matrix products  315 us (20%)
  local copies, waits for them, and re-layouts  203 us (13%)
  starting transfers between devices  94.2 us (6%)
  other arithmetic  77.8 us (5%)
    ppermute x8, waiting for transfers between devices, middle_terms(): received = lax.ppermute(along_two(ends, field), 'narrow', [(1, 0), (2, 3)])  525 us
    dot_general x16, matrix products, along_two(): return jnp.einsum('ij,kjl->kil', matrix, field, precision=HIGH)  176 us
    ppermute x4, waiting for transfers between devices, middle_terms(): lower = lax.ppermute(section, 'narrow', [(0, 1), (1, 2)])  167 us
    ppermute x2, waiting for transfers between devices, two_weights(): ends = lax.ppermute(matrix, 'narrow', [(0, 1), (3, 2)])  91.6 us
    unnamed x38, local copies, waits for them, and re-layouts  81.7 us
    dot_general x4, matrix products, along_one(): return jnp.einsum('ij,jkl->ikl', matrix, field, precision=HIGH)  75.8 us
    dot_general x6, matrix products, along_three(): return jnp.einsum('ij,klj->kli', matrix, field, precision=HIGH)  62.9 us
    all_to_all x4, waiting for transfers between devices, to_whole_one(): lax.all_to_all(blocks, 'wide', split_axis=0, concat_axis=0, tiled=True)  45.7 us
  transfers between devices with their start and end apart: 28, of which 14 were waited for; matrix products, arithmetic and copies ran while one was open for 26% of the time, Pallas kernels for 0%

profile of v2, /device:TPU:0, one launch (start us, length us, event | category | flops | bytes accessed | tf_op | source)
XLA Modules:
  0.0 1544.2 jit_solution(15128099692350465393)
XLA Ops:
  29.8 17.4 %copy.59 = f32[2,64,128,256]{2,3,1,0:T(8,128)} copy(f32[2,64,128,256]{3,2,1,0:T(8,128)} %param.9) | data formatting | bytes 33554432 | tf_op args[0]
  47.3 19.3 %slice_add_fusion.1 = (f32[1,64,128,256]{2,3,1,0:T(8,128)}, f32[1,64,128,256]{2,3,1,0:T(8,128)}) fusion(f32[2,64,128,256]{2,3,1,0:T(8,128)} %copy.59, f32[1,64,128,256]{2,3,1,0:T(8,128)} %copy.100, f32[1,64,128,256]{2,3,1,0:T(8,128)} %copy.101), kind=kLoop, calls=%fused_computation.7 | loop fusion | flops 8388608 | bytes 50331648 | tf_op jit(solution)/shard_map/add | solution.py:78
  112.1 58.5 %collective-permute-done = f32[32,128,256]{1,2,0:T(8,128)} collective-permute-done((f32[32,128,256]{1,2,0:T(8,128)}, f32[32,128,256]{1,2,0:T(8,128)}, u32[]{:S(2)}, u32[]{:S(2)}) %collective-permute-start) | collective-permute-done | bytes 4194336 | tf_op jit(solution)/shard_map/ppermute | solution.py:52
  174.5 84.8 %collective-permute-done.5 = f32[32,128,256]{1,2,0:T(8,128)} collective-permute-done((f32[32,128,256]{1,2,0:T(8,128)}, f32[32,128,256]{1,2,0:T(8,128)}, u32[]{:S(2)}, u32[]{:S(2)}) %collective-permute-start.5) | collective-permute-done | bytes 4194336 | tf_op jit(solution)/shard_map/ppermute | solution.py:52
  284.9 87.7 %collective-permute-done.3 = f32[128,512]{1,0:T(8,128)S(1)} collective-permute-done((f32[128,512]{1,0:T(8,128)S(1)}, f32[128,512]{1,0:T(8,128)S(1)}, u32[]{:S(2)}, u32[]{:S(2)}) %collective-permute-start.3) | collective-permute-done | bytes 262176 | tf_op jit(solution)/shard_map/ppermute | solution.py:44
  414.2 11.7 convolution_bitcast_fusion.7
  427.2 11.7 convolution_bitcast_fusion.6
  448.1 23.8 %collective-permute-done.16 = f32[32,128,256]{1,2,0:T(8,128)} collective-permute-done((f32[32,128,256]{1,2,0:T(8,128)}, f32[32,128,256]{1,2,0:T(8,128)}, u32[]{:S(2)}, u32[]{:S(2)}) %collective-permute-start.16) | collective-permute-done | bytes 4194336 | tf_op jit(solution)/shard_map/ppermute | solution.py:52
  499.9 39.4 %collective-permute-done.4 = f32[32,128,256]{1,2,0:T(8,128)} collective-permute-done((f32[32,128,256]{1,2,0:T(8,128)}, f32[32,128,256]{1,2,0:T(8,128)}, u32[]{:S(2)}, u32[]{:S(2)}) %collective-permute-start.4) | collective-permute-done | bytes 4194336 | tf_op jit(solution)/shard_map/ppermute | solution.py:59
  544.9 80.7 %collective-permute-done.8 = f32[32,128,256]{1,2,0:T(8,128)} collective-permute-done((f32[32,128,256]{1,2,0:T(8,128)}, f32[32,128,256]{1,2,0:T(8,128)}, u32[]{:S(2)}, u32[]{:S(2)}) %collective-permute-start.8) | collective-permute-done | bytes 4194336 | tf_op jit(solution)/shard_map/ppermute | solution.py:59
  657.9 11.7 convolution_bitcast_fusion.2
  691.8 123.7 %collective-permute-done.15 = f32[32,128,256]{1,2,0:T(8,128)S(1)} collective-permute-done((f32[32,128,256]{1,2,0:T(8,128)S(1)}, f32[32,128,256]{1,2,0:T(8,128)S(1)}, u32[]{:S(2)}, u32[]{:S(2)}) %collective-permute-start.15) | collective-permute-done | bytes 4194336 | tf_op jit(solution)/shard_map/ppermute | solution.py:59
  819.0 87.9 %collective-permute-done.19 = f32[32,128,256]{1,2,0:T(8,128)S(1)} collective-permute-done((f32[32,128,256]{1,2,0:T(8,128)}, f32[32,128,256]{1,2,0:T(8,128)S(1)}, u32[]{:S(2)}, u32[]{:S(2)}) %collective-permute-start.19) | collective-permute-done | bytes 4194336 | tf_op jit(solution)/shard_map/ppermute | solution.py:59
  925.2 17.9 %fusion.15 = f32[16,256,512]{2,1,0:T(8,128)S(1)} fusion(f32[512,16,256]{2,1,0:T(8,128)} %bitcast.15, f32[512,512]{1,0:T(8,128)S(1)} %copy-done), kind=kOutput, calls=%fused_computation.30 | convolution fusion | flops 6442450944 | bytes 17825792 | tf_op jit(solution)/shard_map/ij,jkl->ikl/dot_general | solution.py:12
  943.1 20.2 %add_bitcast_fusion.1 = f32[512,16,256]{0,2,1:T(8,128)} fusion(f32[16,256,512]{2,1,0:T(8,128)S(1)} %fusion.15, f32[512,16,256]{2,1,0:T(8,128)} %bitcast.2, f32[512,512]{1,0:T(8,128)S(1)} %copy-done.3), kind=kOutput, calls=%fused_computation.36 | convolution fusion | flops 6444548096 | bytes 26214400 | tf_op jit(solution)/shard_map/ij,jkl->ikl/dot_general | solution.py:12
  973.6 45.7 %all-to-all-done.4 = f32[8,64,16,256]{3,2,1,0:T(8,128)} async-done(((f32[8,64,16,256]{3,2,1,0:T(8,128)}), f32[8,64,16,256]{3,2,1,0:T(8,128)}, u32[]{:S(2)}, u32[]{:S(2)}) %all-to-all-start.4) | async-done | bytes 8388640 | tf_op jit(solution)/shard_map/all_to_all | solution.py:26
  1033.5 11.7 convolution_bitcast_fusion.5
  1046.6 17.8 %fusion.11 = f32[16,256,512]{2,1,0:T(8,128)S(1)} fusion(f32[512,16,256]{2,1,0:T(8,128)} %bitcast.41, f32[512,512]{1,0:T(8,128)S(1)} %copy-done), kind=kOutput, calls=%fused_computation.25 | convolution fusion | flops 6442450944 | bytes 17825792 | tf_op jit(solution)/shard_map/ij,jkl->ikl/dot_general | solution.py:12
  1064.4 20.0 %add_bitcast_fusion = f32[512,16,256]{0,2,1:T(8,128)} fusion(f32[16,256,512]{2,1,0:T(8,128)S(1)} %fusion.11, f32[512,16,256]{2,1,0:T(8,128)} %bitcast.32, f32[512,512]{1,0:T(8,128)S(1)} %copy-done.3), kind=kOutput, calls=%fused_computation.35 | convolution fusion | flops 6444548096 | bytes 26214400 | tf_op jit(solution)/shard_map/ij,jkl->ikl/dot_general | solution.py:12
  1094.6 23.8 %all-to-all-done.2 = f32[8,64,16,256]{3,2,1,0:T(8,128)} async-done(((f32[8,64,16,256]{3,2,1,0:T(8,128)}), f32[8,64,16,256]{3,2,1,0:T(8,128)}, u32[]{:S(2)}, u32[]{:S(2)}) %all-to-all-start.2) | async-done | bytes 8388640 | tf_op jit(solution)/shard_map/all_to_all | solution.py:33
  1123.8 11.7 convolution_bitcast_fusion.4
  1136.8 11.7 convolution_bitcast_fusion.1
  1150.0 11.7 convolution_bitcast_fusion
  1163.1 11.3 fusion.44
  1211.7 19.2 %collective-permute-done.11 = f32[32,128,256]{1,2,0:T(8,128)S(1)} collective-permute-done((f32[32,128,256]{1,2,0:T(8,128)}, f32[32,128,256]{1,2,0:T(8,128)S(1)}, u32[]{:S(2)}, u32[]{:S(2)}) %collective-permute-start.11) | collective-permute-done | bytes 4194336 | tf_op jit(solution)/shard_map/ppermute | solution.py:59
  1233.6 87.3 %collective-permute-done.20 = f32[32,128,256]{1,2,0:T(8,128)S(1)} collective-permute-done((f32[32,128,256]{1,2,0:T(8,128)}, f32[32,128,256]{1,2,0:T(8,128)S(1)}, u32[]{:S(2)}, u32[]{:S(2)}) %collective-permute-start.20) | collective-permute-done | bytes 4194336 | tf_op jit(solution)/shard_map/ppermute | solution.py:59
  1323.5 86.8 %collective-permute-done.21 = f32[32,128,256]{1,2,0:T(8,128)S(1)} collective-permute-done((f32[32,128,256]{1,2,0:T(8,128)}, f32[32,128,256]{1,2,0:T(8,128)S(1)}, u32[]{:S(2)}, u32[]{:S(2)}) %collective-permute-start.21) | collective-permute-done | bytes 4194336 | tf_op jit(solution)/shard_map/ppermute | solution.py:59
  1447.2 21.0 %fusion.1 = f32[1,64,128,256]{2,3,1,0:T(8,128)} fusion(f32[64,128,256]{1,2,0:T(8,128)} %copy.70, f32[32,128,256]{1,2,0:T(8,128)} %bitcast_add_fusion.6, f32[32,128,256]{1,2,0:T(8,128)} %bitcast_add_fusion.7, f32[64,128,256]{1,2,0:T(8,128)} %copy.72, f32[1,64,128,256]{2,3,1,0:T(8,128)} %get-tuple-element.10, f32[256,256]{1,0:T(8,128)S(1)} %copy-done.5), kind=kOutput, calls=%fused_computation.11 | convolution fusion | flops 3231711232 | bytes 42205184 | tf_op jit(solution)/shard_map/ij,klj->kli/dot_general | solution.py:20
  1468.2 19.6 %fusion.4 = f32[1,64,128,256]{2,3,1,0:T(8,128)} fusion(f32[64,128,256]{1,2,0:T(8,128)} %copy.85, f32[32,128,256]{1,2,0:T(8,128)} %bitcast_add_fusion, f32[32,128,256]{1,2,0:T(8,128)S(1)} %copy-done.2, f32[64,128,256]{1,2,0:T(8,128)} %copy.72, f32[1,64,128,256]{2,3,1,0:T(8,128)} %get-tuple-element.11, f32[256,256]{1,0:T(8,128)S(1)} %copy-done.5), kind=kOutput, calls=%fused_computation.16 | convolution fusion | flops 3233808384 | bytes 42205184 | tf_op jit(solution)/shard_map/ij,klj->kli/dot_general | solution.py:20
  1487.9 21.1 %multiply_add_fusion = (f32[2,64,128,256]{2,3,1,0:T(8,128)}, f32[2,64,128,256]{2,3,1,0:T(8,128)}) fusion(f32[2,64,128,256]{2,3,1,0:T(8,128)} %copy.59, f32[1,64,128,256]{2,3,1,0:T(8,128)} %fusion.4, f32[1,64,128,256]{2,3,1,0:T(8,128)} %fusion.1), kind=kLoop, calls=%fused_computation.5 | loop fusion | flops 12582912 | bytes 67108864 | tf_op jit(solution)/shard_map/add | solution.py:91
  1509.0 17.5 %copy.90 = f32[2,64,128,256]{3,2,1,0:T(8,128)} copy(f32[2,64,128,256]{2,3,1,0:T(8,128)} %get-tuple-element.9) | data formatting | bytes 33554432
  1526.5 17.6 %copy.91 = f32[2,64,128,256]{3,2,1,0:T(8,128)} copy(f32[2,64,128,256]{2,3,1,0:T(8,128)} %get-tuple-element.8) | data formatting | bytes 33554432
  (121 shorter events, 391.0 us)
Async XLA Ops:
  0.6 924.6 %copy-start = (f32[512,512]{1,0:T(8,128)S(1)}, f32[512,512]{1,0:T(8,128)}, u32[]{:S(2)}) copy-start(f32[512,512]{1,0:T(8,128)} %param.13) | copy-start | bytes 3145732
  74.3 96.2 %collective-permute-start = (f32[32,128,256]{1,2,0:T(8,128)}, f32[32,128,256]{1,2,0:T(8,128)}, u32[]{:S(2)}, u32[]{:S(2)}) collective-permute-start(f32[32,128,256]{1,2,0:T(8,128)} %get-tuple-element.14), channel_id=1, source_target_pairs={{0,1},{1,2},{4,5},{5,6},{8,9},{9,10},{12,13},{13,14},{16,17},{17,1... | collective-permute-start | bytes 12582920 | tf_op jit(solution)/shard_map/ppermute | solution.py:52
  81.4 89.2 %collective-permute-start.1 = (f32[32,128,256]{1,2,0:T(8,128)}, f32[32,128,256]{1,2,0:T(8,128)}, u32[]{:S(2)}, u32[]{:S(2)}) collective-permute-start(f32[32,128,256]{1,2,0:T(8,128)} %get-tuple-element.14), channel_id=1, source_target_pairs={{3,2},{2,1},{7,6},{6,5},{11,10},{10,9},{15,14},{14,13},{19,18},{18... | collective-permute-start | bytes 12582920 | tf_op jit(solution)/shard_map/ppermute | solution.py:53
  84.0 175.3 %collective-permute-start.5 = (f32[32,128,256]{1,2,0:T(8,128)}, f32[32,128,256]{1,2,0:T(8,128)}, u32[]{:S(2)}, u32[]{:S(2)}) collective-permute-start(f32[32,128,256]{1,2,0:T(8,128)} %get-tuple-element.15), channel_id=1, source_target_pairs={{0,1},{1,2},{4,5},{5,6},{8,9},{9,10},{12,13},{13,14},{16,17},{17,1... | collective-permute-start | bytes 12582920 | tf_op jit(solution)/shard_map/ppermute | solution.py:52
  87.3 172.0 %collective-permute-start.6 = (f32[32,128,256]{1,2,0:T(8,128)}, f32[32,128,256]{1,2,0:T(8,128)}, u32[]{:S(2)}, u32[]{:S(2)}) collective-permute-start(f32[32,128,256]{1,2,0:T(8,128)} %get-tuple-element.15), channel_id=1, source_target_pairs={{3,2},{2,1},{7,6},{6,5},{11,10},{10,9},{15,14},{14,13},{19,18},{18... | collective-permute-start | bytes 12582920 | tf_op jit(solution)/shard_map/ppermute | solution.py:53
  107.1 301.8 %all-to-all-start = ((f32[8,64,16,256]{3,2,1,0:T(8,128)}), f32[8,64,16,256]{3,2,1,0:T(8,128)}, u32[]{:S(2)}, u32[]{:S(2)}) async-start(f32[8,64,16,256]{3,2,1,0:T(8,128)} %copy.62), calls=%async_computation | async-start | bytes 16777216 | tf_op jit(solution)/shard_map/all_to_all | solution.py:26
  170.5 96.2 %slice-start = ((s8[8388608]{0:T(1024)(128)(4,1)}), s8[4194304]{0:T(1024)(128)(4,1)S(1)}, s32[]{:S(2)}) async-start(s8[8388608]{0:T(1024)(128)(4,1)} %bitcast.144), calls=%async_computation.6 | async-start | bytes 8388608
  173.4 93.4 %slice-start.1 = ((s8[8388608]{0:T(1024)(128)(4,1)}), s8[4194304]{0:T(1024)(128)(4,1)S(1)}, s32[]{:S(2)}) async-start(s8[8388608]{0:T(1024)(128)(4,1)} %bitcast.144), calls=%async_computation.7 | async-start | bytes 8388608
  173.4 213.9 %collective-permute-start.2 = (f32[32,128,256]{1,2,0:T(8,128)S(1)}, f32[32,128,256]{1,2,0:T(8,128)S(1)}, u32[]{:S(2)}, u32[]{:S(2)}) collective-permute-start(f32[32,128,256]{1,2,0:T(8,128)S(1)} %broadcast_select_fusion.3), channel_id=1, source_target_pairs={{1,2},{2,1},{5,6},{6,5},{9,10},{10,9},{13,14},{14,13},{17,18},{18,... | collective-permute-start | bytes 12582920 | tf_op jit(solution)/shard_map/ppermute | solution.py:54
  264.1 161.8 %collective-permute-start.7 = (f32[32,128,256]{1,2,0:T(8,128)}, f32[32,128,256]{1,2,0:T(8,128)}, u32[]{:S(2)}, u32[]{:S(2)}) collective-permute-start(f32[32,128,256]{1,2,0:T(8,128)} %broadcast_select_fusion.2), channel_id=1, source_target_pairs={{1,2},{2,1},{5,6},{6,5},{9,10},{10,9},{13,14},{14,13},{17,18},{18,... | collective-permute-start | bytes 12582920 | tf_op jit(solution)/shard_map/ppermute | solution.py:54
  266.8 105.9 %copy-start.7 = (f32[128,512]{1,0:T(8,128)S(1)}, f32[128,512]{1,0:T(8,128)}, u32[]{:S(2)}) copy-start(f32[128,512]{1,0:T(8,128)} %param.14) | copy-start | bytes 786436
  270.6 168.3 %collective-permute-start.12 = (f32[32,128,256]{1,2,0:T(8,128)}, f32[32,128,256]{1,2,0:T(8,128)}, u32[]{:S(2)}, u32[]{:S(2)}) collective-permute-start(f32[32,128,256]{1,2,0:T(8,128)} %get-tuple-element.16), channel_id=1, source_target_pairs={{0,1},{1,2},{4,5},{5,6},{8,9},{9,10},{12,13},{13,14},{16,17},{17,1... | collective-permute-start | bytes 12582920 | tf_op jit(solution)/shard_map/ppermute | solution.py:52
  281.0 159.3 %collective-permute-start.13 = (f32[32,128,256]{1,2,0:T(8,128)}, f32[32,128,256]{1,2,0:T(8,128)}, u32[]{:S(2)}, u32[]{:S(2)}) collective-permute-start(f32[32,128,256]{1,2,0:T(8,128)} %get-tuple-element.16), channel_id=1, source_target_pairs={{3,2},{2,1},{7,6},{6,5},{11,10},{10,9},{15,14},{14,13},{19,18},{18... | collective-permute-start | bytes 12582920 | tf_op jit(solution)/shard_map/ppermute | solution.py:53
  283.6 89.0 %collective-permute-start.3 = (f32[128,512]{1,0:T(8,128)S(1)}, f32[128,512]{1,0:T(8,128)S(1)}, u32[]{:S(2)}, u32[]{:S(2)}) collective-permute-start(f32[128,512]{1,0:T(8,128)S(1)} %copy-done.6), channel_id=1, source_target_pairs={{0,1},{3,2},{4,5},{7,6},{8,9},{11,10},{12,13},{15,14},{16,17},{19,... | collective-permute-start | bytes 786440 | tf_op jit(solution)/shard_map/ppermute | solution.py:44
  372.6 8.3 collective-permute-start.9
  380.9 91.0 %collective-permute-start.16 = (f32[32,128,256]{1,2,0:T(8,128)}, f32[32,128,256]{1,2,0:T(8,128)}, u32[]{:S(2)}, u32[]{:S(2)}) collective-permute-start(f32[32,128,256]{1,2,0:T(8,128)} %get-tuple-element.17), channel_id=1, source_target_pairs={{0,1},{1,2},{4,5},{5,6},{8,9},{9,10},{12,13},{13,14},{16,17},{17,1... | collective-permute-start | bytes 12582920 | tf_op jit(solution)/shard_map/ppermute | solution.py:52
  389.3 82.6 %collective-permute-start.17 = (f32[32,128,256]{1,2,0:T(8,128)}, f32[32,128,256]{1,2,0:T(8,128)}, u32[]{:S(2)}, u32[]{:S(2)}) collective-permute-start(f32[32,128,256]{1,2,0:T(8,128)} %get-tuple-element.17), channel_id=1, source_target_pairs={{3,2},{2,1},{7,6},{6,5},{11,10},{10,9},{15,14},{14,13},{19,18},{18... | collective-permute-start | bytes 12582920 | tf_op jit(solution)/shard_map/ppermute | solution.py:53
  408.9 231.8 %all-to-all-start.3 = ((f32[8,64,16,256]{3,2,1,0:T(8,128)}), f32[8,64,16,256]{3,2,1,0:T(8,128)}, u32[]{:S(2)}, u32[]{:S(2)}) async-start(f32[8,64,16,256]{3,2,1,0:T(8,128)} %copy.77), calls=%async_computation.3 | async-start | bytes 16777216 | tf_op jit(solution)/shard_map/all_to_all | solution.py:26
  425.9 113.4 %collective-permute-start.4 = (f32[32,128,256]{1,2,0:T(8,128)}, f32[32,128,256]{1,2,0:T(8,128)}, u32[]{:S(2)}, u32[]{:S(2)}) collective-permute-start(f32[32,128,256]{1,2,0:T(8,128)} %convolution_bitcast_fusion.7), channel_id=1, source_target_pairs={{1,0},{2,3},{5,4},{6,7},{9,8},{10,11},{13,12},{14,15},{17,16},{18,... | collective-permute-start | bytes 12582920 | tf_op jit(solution)/shard_map/ppermute | solution.py:59
  438.9 186.7 %collective-permute-start.8 = (f32[32,128,256]{1,2,0:T(8,128)}, f32[32,128,256]{1,2,0:T(8,128)}, u32[]{:S(2)}, u32[]{:S(2)}) collective-permute-start(f32[32,128,256]{1,2,0:T(8,128)} %convolution_bitcast_fusion.6), channel_id=1, source_target_pairs={{1,0},{2,3},{5,4},{6,7},{9,8},{10,11},{13,12},{14,15},{17,16},{18,... | collective-permute-start | bytes 12582920 | tf_op jit(solution)/shard_map/ppermute | solution.py:59
  445.2 200.4 %collective-permute-start.14 = (f32[32,128,256]{1,2,0:T(8,128)}, f32[32,128,256]{1,2,0:T(8,128)}, u32[]{:S(2)}, u32[]{:S(2)}) collective-permute-start(f32[32,128,256]{1,2,0:T(8,128)} %broadcast_select_fusion.1), channel_id=1, source_target_pairs={{1,2},{2,1},{5,6},{6,5},{9,10},{10,9},{13,14},{14,13},{17,18},{18,... | collective-permute-start | bytes 12582920 | tf_op jit(solution)/shard_map/ppermute | solution.py:54
  476.7 181.2 %collective-permute-start.18 = (f32[32,128,256]{1,2,0:T(8,128)}, f32[32,128,256]{1,2,0:T(8,128)}, u32[]{:S(2)}, u32[]{:S(2)}) collective-permute-start(f32[32,128,256]{1,2,0:T(8,128)} %broadcast_select_fusion), channel_id=1, source_target_pairs={{1,2},{2,1},{5,6},{6,5},{9,10},{10,9},{13,14},{14,13},{17,18},{18,... | collective-permute-start | bytes 12582920 | tf_op jit(solution)/shard_map/ppermute | solution.py:54
  640.7 279.2 %all-to-all-start.1 = ((f32[8,64,16,256]{3,2,1,0:T(8,128)}), f32[8,64,16,256]{3,2,1,0:T(8,128)}, u32[]{:S(2)}, u32[]{:S(2)}) async-start(f32[8,64,16,256]{3,2,1,0:T(8,128)} %bitcast.147), calls=%async_computation.1 | async-start | bytes 16777216 | tf_op jit(solution)/shard_map/all_to_all | solution.py:26
  656.1 159.5 %collective-permute-start.15 = (f32[32,128,256]{1,2,0:T(8,128)S(1)}, f32[32,128,256]{1,2,0:T(8,128)S(1)}, u32[]{:S(2)}, u32[]{:S(2)}) collective-permute-start(f32[32,128,256]{1,2,0:T(8,128)S(1)} %convolution_bitcast_fusion.3), channel_id=1, source_target_pairs={{1,0},{2,3},{5,4},{6,7},{9,8},{10,11},{13,12},{14,15},{17,16},{18,... | collective-permute-start | bytes 12582920 | tf_op jit(solution)/shard_map/ppermute | solution.py:59
  669.7 237.2 %collective-permute-start.19 = (f32[32,128,256]{1,2,0:T(8,128)}, f32[32,128,256]{1,2,0:T(8,128)S(1)}, u32[]{:S(2)}, u32[]{:S(2)}) collective-permute-start(f32[32,128,256]{1,2,0:T(8,128)} %convolution_bitcast_fusion.2), channel_id=1, source_target_pairs={{1,0},{2,3},{5,4},{6,7},{9,8},{10,11},{13,12},{14,15},{17,16},{18,... | collective-permute-start | bytes 12582920 | tf_op jit(solution)/shard_map/ppermute | solution.py:59
  920.0 99.3 %all-to-all-start.4 = ((f32[8,64,16,256]{3,2,1,0:T(8,128)}), f32[8,64,16,256]{3,2,1,0:T(8,128)}, u32[]{:S(2)}, u32[]{:S(2)}) async-start(f32[8,64,16,256]{3,2,1,0:T(8,128)} %bitcast.149), calls=%async_computation.4 | async-start | bytes 16777216 | tf_op jit(solution)/shard_map/all_to_all | solution.py:26
  1019.3 99.2 %all-to-all-start.2 = ((f32[8,64,16,256]{3,2,1,0:T(8,128)}), f32[8,64,16,256]{3,2,1,0:T(8,128)}, u32[]{:S(2)}, u32[]{:S(2)}) async-start(f32[8,64,16,256]{3,2,1,0:T(8,128)} %bitcast.148), calls=%async_computation.2 | async-start | bytes 16777216 | tf_op jit(solution)/shard_map/all_to_all | solution.py:33
  1045.3 160.3 %collective-permute-start.10 = (f32[32,128,256]{1,2,0:T(8,128)}, f32[32,128,256]{1,2,0:T(8,128)}, u32[]{:S(2)}, u32[]{:S(2)}) collective-permute-start(f32[32,128,256]{1,2,0:T(8,128)} %convolution_bitcast_fusion.5), channel_id=1, source_target_pairs={{1,0},{2,3},{5,4},{6,7},{9,8},{10,11},{13,12},{14,15},{17,16},{18,... | collective-permute-start | bytes 12582920 | tf_op jit(solution)/shard_map/ppermute | solution.py:59
  1118.4 311.6 %all-to-all-start.5 = ((f32[8,64,16,256]{3,2,1,0:T(8,128)}), f32[8,64,16,256]{3,2,1,0:T(8,128)}, u32[]{:S(2)}, u32[]{:S(2)}) async-start(f32[8,64,16,256]{3,2,1,0:T(8,128)} %bitcast.146), calls=%async_computation.5 | async-start | bytes 16777216 | tf_op jit(solution)/shard_map/all_to_all | solution.py:33
  1135.5 95.5 %collective-permute-start.11 = (f32[32,128,256]{1,2,0:T(8,128)}, f32[32,128,256]{1,2,0:T(8,128)S(1)}, u32[]{:S(2)}, u32[]{:S(2)}) collective-permute-start(f32[32,128,256]{1,2,0:T(8,128)} %convolution_bitcast_fusion.4), channel_id=1, source_target_pairs={{1,0},{2,3},{5,4},{6,7},{9,8},{10,11},{13,12},{14,15},{17,16},{18,... | collective-permute-start | bytes 12582920 | tf_op jit(solution)/shard_map/ppermute | solution.py:59
  1148.5 172.4 %collective-permute-start.20 = (f32[32,128,256]{1,2,0:T(8,128)}, f32[32,128,256]{1,2,0:T(8,128)S(1)}, u32[]{:S(2)}, u32[]{:S(2)}) collective-permute-start(f32[32,128,256]{1,2,0:T(8,128)} %convolution_bitcast_fusion.1), channel_id=1, source_target_pairs={{1,0},{2,3},{5,4},{6,7},{9,8},{10,11},{13,12},{14,15},{17,16},{18,... | collective-permute-start | bytes 12582920 | tf_op jit(solution)/shard_map/ppermute | solution.py:59
  1161.8 248.5 %collective-permute-start.21 = (f32[32,128,256]{1,2,0:T(8,128)}, f32[32,128,256]{1,2,0:T(8,128)S(1)}, u32[]{:S(2)}, u32[]{:S(2)}) collective-permute-start(f32[32,128,256]{1,2,0:T(8,128)} %convolution_bitcast_fusion), channel_id=1, source_target_pairs={{1,0},{2,3},{5,4},{6,7},{9,8},{10,11},{13,12},{14,15},{17,16},{18,... | collective-permute-start | bytes 12582920 | tf_op jit(solution)/shard_map/ppermute | solution.py:59
  (12 other events, 256.1 us)
